TPU v7x, 32 devices: a whole 2x2x4 slice. The times are simulated.
32 devices in a mesh: expert: 16 (over z, x, core), tensor: 2 (over y).
Axes of the slice: x: 2, y: 2, z: 4, core: 2. Of those that a mesh axis runs over, the one named last changes fastest.
Arguments:
- attn_out: bfloat16 [2048, 4096], P('expert', 'tensor'), may hold values from -6 to 6
- residual: bfloat16 [2048, 4096], P('expert'), may hold values from -6 to 6
- o_weight: bfloat16 [4096, 4096], P('tensor'), may hold values from -0.09375 to 0.09375
- norm_gain: float32 [4096], replicated, may hold values from 0.5 to 1.5
- router_weight: bfloat16 [4096, 16], replicated, may hold values from -0.09375 to 0.09375
- expert_idx: int32 [2048, 8], P('expert'), may hold values from 0 to 15, all different within a row; in each aligned block of 64 rows (0 to 63, 64 to 127, ...) at most 48 rows name the same one
- combine: float32 [2048, 8], P('expert'), may hold values from 0.05 to 0.25
- w_gate: bfloat16 [16, 4096, 1536], P('expert', None, 'tensor'), may hold values from -0.09375 to 0.09375
- w_up: bfloat16 [16, 4096, 1536], P('expert', None, 'tensor'), may hold values from -0.09375 to 0.09375
- w_down: bfloat16 [16, 1536, 4096], P('expert', 'tensor'), may hold values from -0.15625 to 0.15625
Outputs:
- mixed: bfloat16 [2048, 4096], P('expert')
- router_logits: float32 [2048, 16], P('expert')
Inputs may be any that keep to these rules, and one draw needn't show every extreme that they name: `expert_idx`: each row names 8 different experts. In each aligned block of 64 tokens no expert is named by more than 48 tokens, a bound that some block reaches.
All inputs are finite; a program needn't handle non-finite values.
Results may differ from a plain program's by a relative error of at most 0.015.
Values may be sent and summed in bfloat16 or wider, within the bound.
A program may use at most 128 MiB of HBM per device.

v0:
```python
import jax
import jax.numpy as jnp
from jax import lax
from jax.sharding import PartitionSpec as P

epsilon = 1e-06


def rms_scaled(stream, norm_gain):
    stream_wide = stream.astype(jnp.float32)
    scale = lax.rsqrt(jnp.mean(stream_wide * stream_wide, axis=-1, keepdims=True) + epsilon)
    return (stream_wide * scale * norm_gain).astype(jnp.bfloat16)


def slot_targets(chosen, expert_count, capacity):
    flat_ids = chosen.reshape(-1)
    one_hot = (flat_ids[:, None] == jnp.arange(expert_count, dtype=jnp.int32)[None, :]).astype(
        jnp.int32
    )
    slot_index = jnp.sum((jnp.cumsum(one_hot, axis=0) - 1) * one_hot, axis=1)
    return (flat_ids * capacity + slot_index).reshape(chosen.shape)


def selector(targets, slot_total):
    slots = jnp.arange(slot_total, dtype=jnp.int32)
    hits = jnp.any(slots[:, None, None] == targets[None, :, :], axis=2)
    return hits.astype(jnp.bfloat16)


def expert_hidden(rows_in, w_gate, w_up):
    flat_rows = rows_in.reshape(-1, rows_in.shape[-1])
    gate = jnp.dot(flat_rows, w_gate[0], preferred_element_type=jnp.float32)
    up_val = jnp.dot(flat_rows, w_up[0], preferred_element_type=jnp.float32)
    return (jax.nn.silu(gate) * up_val).astype(jnp.bfloat16)


def shards(
    attn_out,
    residual,
    o_weight,
    norm_gain,
    router_weight,
    expert_idx,
    combine,
    w_gate,
    w_up,
    w_down,
):
    tensor_size = lax.axis_size("tensor")
    tensor_rank = lax.axis_index("tensor")
    group_rows = residual.shape[0]
    width = residual.shape[1]
    rows_dev = group_rows // tensor_size
    expert_count = router_weight.shape[1]
    top_count = expert_idx.shape[1]
    capacity = min(rows_dev, max(2, 3 * rows_dev * top_count // (2 * expert_count)))
    slot_total = expert_count * capacity
    offset_mine = tensor_rank * rows_dev
    my_chosen = lax.dynamic_slice_in_dim(expert_idx, offset_mine, rows_dev, 0)
    my_combine = lax.dynamic_slice_in_dim(combine, offset_mine, rows_dev, 0)
    my_target = slot_targets(my_chosen, expert_count, capacity)
    rows_in = attn_out
    projected = lax.psum_scatter(
        jnp.dot(rows_in, o_weight, preferred_element_type=jnp.float32).astype(jnp.bfloat16),
        "tensor",
        scatter_dimension=0,
        tiled=True,
    ).astype(jnp.float32)
    residual_mine = lax.dynamic_slice_in_dim(residual, offset_mine, rows_dev, 0)
    stream = (residual_mine.astype(jnp.float32) + projected).astype(jnp.bfloat16)
    normed = rms_scaled(stream, norm_gain)
    outbox = jnp.dot(
        selector(my_target, slot_total), normed, preferred_element_type=jnp.float32
    ).astype(jnp.bfloat16)
    arrived = lax.all_to_all(
        outbox.reshape(expert_count, capacity, width),
        "expert",
        split_axis=0,
        concat_axis=0,
        tiled=True,
    )
    hidden = expert_hidden(
        lax.all_gather(arrived[None], "tensor", axis=0, tiled=True), w_gate, w_up
    )
    router_logits = jnp.dot(normed, router_weight, preferred_element_type=jnp.float32)
    rows_in = hidden
    summed = lax.psum_scatter(
        jnp.dot(rows_in, w_down[0], preferred_element_type=jnp.float32).astype(jnp.bfloat16),
        "tensor",
        scatter_dimension=0,
        tiled=True,
    )
    expert_out = summed.reshape(expert_count, capacity, width)
    returned = lax.all_to_all(
        expert_out, "expert", split_axis=0, concat_axis=0, tiled=True
    ).reshape(slot_total, width)
    slots = jnp.arange(slot_total, dtype=jnp.int32)
    weight_matrix = jnp.sum(
        my_combine[:, :, None]
        * (my_target[:, :, None] == slots[None, None, :]).astype(jnp.float32),
        axis=1,
    )
    moe = jnp.dot(weight_matrix, returned.astype(jnp.float32), precision=lax.Precision.HIGHEST)
    mixed = (stream.astype(jnp.float32) + moe).astype(jnp.bfloat16)
    mixed_group, logits_group = (
        lax.all_gather(
            mixed.astype(jnp.float32).astype(jnp.bfloat16), "tensor", axis=0, tiled=True
        ).astype(jnp.float32),
        lax.all_gather(router_logits.astype(jnp.bfloat16), "tensor", axis=0, tiled=True).astype(
            router_logits.dtype
        ),
    )
    return (mixed_group.astype(jnp.bfloat16), logits_group)


def solution(mesh):
    in_specs = (
        P("expert", "tensor"),
        P("expert", None),
        P("tensor", None),
        P(),
        P(),
        P("expert", None),
        P("expert", None),
        P("expert", None, "tensor"),
        P("expert", None, "tensor"),
        P("expert", "tensor", None),
    )
    out_specs = (P("expert", None), P("expert", None))
    return jax.shard_map(shards, mesh=mesh, in_specs=in_specs, out_specs=out_specs, check_vma=False)
```

profile of v0, /device:TPU:0, one launch (start us, length us, event | category | flops | bytes accessed | tf_op | source)
XLA Modules:
  0.0 705.5 jit_solution(8417828719087738778)
XLA Ops:
  7.2 0.0 copy-start
  7.2 0.0 copy-start.4
  7.2 0.0 copy-start.2
  7.2 0.0 copy-start.3
  7.2 0.0 reduce-scatter.3.cloned.1.call-start
  7.3 1.0 copy-done
  8.2 9.1 %convolution_convert_fusion.2 = bf16[128,4096]{1,0:T(8,128)(2,1)} fusion(bf16[128,2048]{1,0:T(8,128)(2,1)S(1)} %copy-done, bf16[2048,4096]{1,0:T(8,128)(2,1)} %param.12), kind=kOutput, calls=%fused_computation.7 | convolution fusion | flops 2148007936 | bytes 18350080 | tf_op jit(solution)/shard_map/dot_general | solution.py:64
  17.3 0.0 reduce-scatter.3.cloned.1.call-update
  17.3 0.0 all-gather.7.cloned.1.call-start
  17.4 0.0 copy-done.4
  17.4 0.1 constant_dynamic-slice_fusion.1
  17.5 0.1 copy.27
  17.5 0.1 eq.55
  17.6 0.1 eq.51
  17.7 1.2 reduce-window.6
  18.9 0.2 slice_reduce_fusion
  19.2 0.1 fusion.16
  19.3 0.1 reduce_sum.30
  19.4 0.5 fusion.8
  19.9 20.6 %reduce-scatter.3.cloned.1.call-done = bf16[64,4096]{1,0:T(8,128)(2,1)} async-done(((bf16[128,4096]{1,0:T(8,128)(2,1)}), bf16[64,4096]{1,0:T(8,128)(2,1)}) %reduce-scatter.3.cloned.1.call-update) | async-done | bytes 524304 | tf_op jit(solution)/shard_map/reduce_scatter | solution.py:63
  40.5 0.0 copy-done.2
  40.5 1.3 fusion.10
  41.8 0.0 copy-done.3
  41.8 1.9 convolution_convert_fusion.1
  43.7 142.7 %all_to_all.10 = bf16[16,48,4096]{2,1,0:T(8,128)(2,1)} all-to-all(bf16[16,48,4096]{2,1,0:T(8,128)(2,1)S(1)} %bitcast.43), channel_id=1, replica_groups=mesh['expert'=16,'tensor'=2] {'expert'}, dimensions={0} | all-to-all | bytes 12582912 | tf_op jit(solution)/shard_map/all_to_all | solution.py:75
  186.4 0.0 all-gather.7.cloned.1.call-update
  186.5 0.2 reduce-scatter.5.cloned.1.call-start
  186.7 152.3 %all-gather.7.cloned.1.call-done = bf16[32,48,4096]{2,1,0:T(8,128)(2,1)} async-done(((bf16[16,48,4096]{2,1,0:T(8,128)(2,1)}), bf16[32,48,4096]{2,1,0:T(8,128)(2,1)}) %all-gather.7.cloned.1.call-update) | async-done | bytes 12582928 | tf_op jit(solution)/shard_map/all_gather | solution.py:83
  339.0 0.0 copy-start.6
  339.0 0.0 slice-start
  339.0 16.2 %fusion.1 = f32[1536,768]{1,0:T(8,128)} fusion(bf16[1536,4096]{1,0:T(8,128)(2,1)} %bitcast.45, bf16[1,4096,768]{2,1,0:T(8,128)(2,1)} %param.18), kind=kOutput, calls=%fused_computation.3 | convolution fusion | flops 9663676416 | bytes 23592960 | tf_op jit(solution)/shard_map/dot_general | solution.py:33
  355.2 0.0 copy-done.6
  355.2 0.0 slice-start.1
  355.2 13.5 %multiply_convert_fusion = bf16[1536,768]{1,0:T(8,128)(2,1)S(1)} fusion(f32[1536,768]{1,0:T(8,128)} %fusion.1, bf16[1536,4096]{1,0:T(8,128)(2,1)S(1)} %bitcast.46, bf16[1,4096,768]{2,1,0:T(8,128)(2,1)} %param.17), kind=kOutput, calls=%fused_computation.8 | convolution fusion | flops 9670754304 | bytes 25952256 | tf_op jit(solution)/shard_map/dot_general | solution.py:32
  368.7 0.0 slice-done
  368.8 0.0 slice-done.1
  368.8 12.3 %convolution_convert_fusion = bf16[1536,4096]{1,0:T(8,128)(2,1)} fusion(bf16[1536,768]{1,0:T(8,128)(2,1)S(1)} %multiply_convert_fusion, bf16[1,768,4096]{2,1,0:T(8,128)(2,1)S(1)} %bitcast.48), kind=kOutput, calls=%fused_computation | convolution fusion | flops 9669967872 | bytes 21233664 | tf_op jit(solution)/shard_map/dot_general | solution.py:88
  381.1 0.0 reduce-scatter.5.cloned.1.call-update
  381.1 144.6 %reduce-scatter.5.cloned.1.call-done = bf16[768,4096]{1,0:T(8,128)(2,1)} async-done(((bf16[1536,4096]{1,0:T(8,128)(2,1)}), bf16[768,4096]{1,0:T(8,128)(2,1)}) %reduce-scatter.5.cloned.1.call-update) | async-done | bytes 6291472 | tf_op jit(solution)/shard_map/reduce_scatter | solution.py:87
  525.7 0.0 copy-start.5
  525.7 5.8 all-to-all-start.1
  531.5 0.0 copy-start.7
  531.5 0.0 copy-start.1
  531.6 0.3 all-gather.5.cloned.1.call-start
  531.8 0.0 copy-done.5
  531.8 0.1 constant_dynamic-slice_fusion
  531.9 0.1 copy.25
  532.0 0.5 select_reduce_fusion
  532.6 113.2 %all-to-all-done.1 = bf16[16,48,4096]{2,1,0:T(8,128)(2,1)} async-done(((bf16[16,48,4096]{2,1,0:T(8,128)(2,1)}), bf16[16,48,4096]{2,1,0:T(8,128)(2,1)}, u32[]{:S(2)}, u32[]{:S(2)}) %all-to-all-start.1) | async-done | bytes 6291488 | tf_op jit(solution)/shard_map/all_to_all | solution.py:94
  645.7 7.0 fusion.5
  652.7 0.0 all-gather.5.cloned.1.call-update
  652.7 0.0 copy-done.7
  652.7 0.3 fusion.9
  653.1 4.3 all-gather.1
  657.4 0.7 reshape.67
  658.1 38.6 %all-gather.5.cloned.1.call-done = bf16[128,4096]{1,0:T(8,128)(2,1)} async-done(((bf16[64,4096]{1,0:T(8,128)(2,1)}), bf16[128,4096]{1,0:T(8,128)(2,1)}) %all-gather.5.cloned.1.call-update) | async-done | bytes 1048592 | tf_op jit(solution)/shard_map/all_gather | solution.py:106
  696.6 2.3 copy.31
  698.9 0.0 copy-done.1
  (7 shorter events, 0.1 us)
Async XLA Ops:
  7.2 1.1 copy-start
  7.2 10.2 %copy-start.4 = (s32[128,8]{0,1:T(8,128)S(1)}, s32[128,8]{0,1:T(8,128)}, u32[]{:S(2)}) copy-start(s32[128,8]{0,1:T(8,128)} %param.15) | copy-start | bytes 12292
  7.2 33.3 %copy-start.2 = (bf16[128,4096]{1,0:T(8,128)(2,1)S(1)}, bf16[128,4096]{1,0:T(8,128)(2,1)}, u32[]{:S(2)}) copy-start(bf16[128,4096]{1,0:T(8,128)(2,1)} %param.11) | copy-start | bytes 3145732
  7.2 34.6 %copy-start.3 = (f32[4096]{0:T(1024)S(1)}, f32[4096]{0:T(1024)}, u32[]{:S(2)}) copy-start(f32[4096]{0:T(1024)} %param.13) | copy-start | bytes 49156
  7.2 33.3 %reduce-scatter.3.cloned.1.call-start = ((), (), s32[]{:S(2)}) async-start(), calls=%async_computation.4 | async-start | bytes 1572864 | tf_op jit(solution)/shard_map/reduce_scatter | solution.py:63
  17.3 321.7 %all-gather.7.cloned.1.call-start = ((), (), s32[]{:S(2)}) async-start(), calls=%async_computation.7 | async-start | bytes 18874368 | tf_op jit(solution)/shard_map/all_gather | solution.py:83
  186.5 339.3 %reduce-scatter.5.cloned.1.call-start = ((), (), s32[]{:S(2)}) async-start(), calls=%async_computation.5 | async-start | bytes 18874368 | tf_op jit(solution)/shard_map/reduce_scatter | solution.py:87
  339.0 16.2 %copy-start.6 = (bf16[32,48,4096]{2,1,0:T(8,128)(2,1)S(1)}, bf16[32,48,4096]{2,1,0:T(8,128)(2,1)}, u32[]{:S(2)}) copy-start(bf16[32,48,4096]{2,1,0:T(8,128)(2,1)} %all-gather.7.cloned.1.call-done) | copy-start | bytes 37748740
  339.0 29.7 %slice-start = ((s8[6291456]{0:T(1024)(128)(4,1)}), s8[4194304]{0:T(1024)(128)(4,1)S(1)}, s32[]{:S(2)}) async-start(s8[6291456]{0:T(1024)(128)(4,1)} %bitcast.47), calls=%async_computation.8 | async-start | bytes 8388608
  355.2 13.5 %slice-start.1 = ((s8[6291456]{0:T(1024)(128)(4,1)}), s8[2097152]{0:T(1024)(128)(4,1)S(1)}, s32[]{:S(2)}) async-start(s8[6291456]{0:T(1024)(128)(4,1)} %bitcast.47), calls=%async_computation.9 | async-start | bytes 4194304
  525.7 6.1 copy-start.5
  525.7 120.0 %all-to-all-start.1 = ((bf16[16,48,4096]{2,1,0:T(8,128)(2,1)}), bf16[16,48,4096]{2,1,0:T(8,128)(2,1)}, u32[]{:S(2)}, u32[]{:S(2)}) async-start(bf16[16,48,4096]{2,1,0:T(8,128)(2,1)} %bitcast.44), calls=%async_computation.3 | async-start | bytes 12582912 | tf_op jit(solution)/shard_map/all_to_all | solution.py:94
  531.5 121.2 %copy-start.7 = (bf16[4096,16]{0,1:T(8,128)(2,1)S(1)}, bf16[4096,16]{0,1:T(8,128)(2,1)}, u32[]{:S(2)}) copy-start(bf16[4096,16]{0,1:T(8,128)(2,1)} %param.14) | copy-start | bytes 393220
  531.5 167.4 %copy-start.1 = (bf16[128,2048]{1,0:T(8,128)(2,1)S(1)}, bf16[128,2048]{1,0:T(8,128)(2,1)}, u32[]{:S(2)}) copy-start(bf16[128,2048]{1,0:T(8,128)(2,1)} %param.10) | copy-start | bytes 1572868
  531.6 165.1 %all-gather.5.cloned.1.call-start = ((), (), s32[]{:S(2)}) async-start(), calls=%async_computation.6 | async-start | bytes 1572864 | tf_op jit(solution)/shard_map/all_gather | solution.py:106
Sparse Core Ops, SparseCore 0:
  17.4 22.9 reduce-scatter.2
  186.6 152.3 all-gather.6
  381.2 144.4 reduce-scatter.4
  652.8 43.7 all-gather.4
where the time goes:
time: 706 us; the launch traced here: 705 us
  waiting for transfers between devices  469 us (66%)
  blocking collectives  147 us (21%)
  matrix products  60.2 us (9%)
  between operations  14 us (2%)
    all_gather x1, waiting for transfers between devices, shards(): lax.all_gather(arrived[None], 'tensor', axis=0, tiled=True)  152 us
    reduce_scatter x1, waiting for transfers between devices, shards(): lax.psum_scatter(jnp.dot(rows_in, w_down[0], preferred_element_type=jnp.f...  145 us
    all_to_all x1, blocking collectives, shards(): lax.all_to_all(outbox.reshape(expert_count, capacity, width), 'expert', s...  143 us
    all_to_all x1, waiting for transfers between devices, shards(): lax.all_to_all(expert_out, 'expert', split_axis=0, concat_axis=0, tiled=T...  113 us
    all_gather x1, waiting for transfers between devices, shards(): lax.all_gather(mixed.astype(jnp.float32).astype(jnp.bfloat16), 'tensor',...  38.6 us
    reduce_scatter x1, waiting for transfers between devices, shards(): lax.psum_scatter(jnp.dot(rows_in, o_weight, preferred_element_type=jnp.fl...  20.6 us
    dot_general x1, matrix products, expert_hidden(): up_val = jnp.dot(flat_rows, w_up[0], preferred_element_type=jnp.float32)  16.2 us
  transfers between devices with their start and end apart: 5, of which 5 were waited for; matrix products, arithmetic and copies ran while one was open for 1% of the time, Pallas kernels for 0%

commit v1 on v0

v1 whole, which is shorter than its diff:
```python
import jax
import jax.numpy as jnp
from jax import lax
from jax.sharding import PartitionSpec as P

epsilon = 1e-06


def rms_scaled(stream, norm_gain):
    wide = stream.astype(jnp.float32)
    scale = lax.rsqrt(jnp.mean(wide * wide, axis=-1, keepdims=True) + epsilon)
    return (wide * scale * norm_gain).astype(jnp.bfloat16)


def shards(
    attn_out,
    residual,
    o_weight,
    norm_gain,
    router_weight,
    expert_idx,
    combine,
    w_gate,
    w_up,
    w_down,
):
    tensor_size = lax.axis_size("tensor")
    tensor_rank = lax.axis_index("tensor")
    me = lax.axis_index("expert")
    rows_dev = residual.shape[0] // tensor_size
    expert_count = router_weight.shape[1]
    experts = jnp.arange(expert_count, dtype=jnp.int32)
    dense = jnp.sum(
        jnp.where(expert_idx[:, :, None] == experts, combine[:, :, None], 0.0), axis=1
    )
    dense_all = lax.all_gather(dense, "expert", axis=0, tiled=True)
    mine = jnp.sum(jnp.where(experts == me, dense_all, 0.0), axis=1, keepdims=True)

    projected = lax.psum_scatter(
        jnp.dot(attn_out, o_weight, preferred_element_type=jnp.float32).astype(jnp.bfloat16),
        "tensor",
        scatter_dimension=0,
        tiled=True,
    ).astype(jnp.float32)
    residual_mine = lax.dynamic_slice_in_dim(residual, tensor_rank * rows_dev, rows_dev, 0)
    stream = (residual_mine.astype(jnp.float32) + projected).astype(jnp.bfloat16)
    normed = rms_scaled(stream, norm_gain)
    every = lax.all_gather(normed, ("expert", "tensor"), axis=0, tiled=True)
    logits = jnp.dot(normed, router_weight, preferred_element_type=jnp.float32)
    gate = jnp.dot(every, w_gate[0], preferred_element_type=jnp.float32)
    up = jnp.dot(every, w_up[0], preferred_element_type=jnp.float32)
    hidden = (jax.nn.silu(gate) * up * mine).astype(jnp.bfloat16)
    part = jnp.dot(hidden, w_down[0], preferred_element_type=jnp.float32).astype(jnp.bfloat16)
    moe = lax.psum_scatter(part, ("expert", "tensor"), scatter_dimension=0, tiled=True)
    mixed = (stream.astype(jnp.float32) + moe.astype(jnp.float32)).astype(jnp.bfloat16)
    return (
        lax.all_gather(mixed, "tensor", axis=0, tiled=True),
        lax.all_gather(logits, "tensor", axis=0, tiled=True),
    )


def solution(mesh):
    in_specs = (
        P("expert", "tensor"),
        P("expert", None),
        P("tensor", None),
        P(),
        P(),
        P("expert", None),
        P("expert", None),
        P("expert", None, "tensor"),
        P("expert", None, "tensor"),
        P("expert", "tensor", None),
    )
    out_specs = (P("expert", None), P("expert", None))
    return jax.shard_map(shards, mesh=mesh, in_specs=in_specs, out_specs=out_specs, check_vma=False)
```

time: 706 us -> 608 us (0.86)
  blocking collectives: 147 us -> 26.6 us
  waiting for transfers between devices: 469 us -> 490 us
  matrix products: 60.2 us -> 68 us
    reduce_scatter x2, waiting for transfers between devices: 165 us -> 379 us  [the longest x1 356 us: shards(): lax.psum_scatter(part, ('expert', 'tensor'), scatter_dimension=0, tiled=T...]
    all_to_all x1 -> x0, blocking collectives: 143 us -> none  [shards(): lax.all_to_all(outbox.reshape(expert_count, capacity, width), 'expert', s...]
    all_to_all x1 -> x0, waiting for transfers between devices: 113 us -> none  [shards(): lax.all_to_all(expert_out, 'expert', split_axis=0, concat_axis=0, tiled=T...]
    all_gather x2, waiting for transfers between devices: 191 us -> 111 us  [the longest x1 94.1 us: shards(): every = lax.all_gather(normed, ('expert', 'tensor'), axis=0, tiled=True)]
    all_gather x1 -> x2, blocking collectives: 4.34 us -> 26.6 us  [the longest x1 22.2 us: shards(): dense_all = lax.all_gather(dense, 'expert', axis=0, tiled=True)]
    dot_general x7 -> x5, matrix products: 60.2 us -> 68 us  [the longest x1 21.4 us: shards(): gate = jnp.dot(every, w_gate[0], preferred_element_type=jnp.float32)]
  transfers between devices with their start and end apart: 5 -> 4, of which waited for: 5 -> 4; matrix products, arithmetic and copies ran while one was open for 1% -> 0% of each run, Pallas kernels for 0% -> 0%
where the time goes in v1:
time: 608 us; the launch traced here: 607 us
  waiting for transfers between devices  490 us (81%)
  matrix products  68 us (11%)
  blocking collectives  26.6 us (4%)
  between operations  13.9 us (2%)
    reduce_scatter x1, waiting for transfers between devices, shards(): lax.psum_scatter(part, ('expert', 'tensor'), scatter_dimension=0, tiled=T...  356 us
    all_gather x1, waiting for transfers between devices, shards(): every = lax.all_gather(normed, ('expert', 'tensor'), axis=0, tiled=True)  94.1 us
    reduce_scatter x1, waiting for transfers between devices, shards(): lax.psum_scatter(jnp.dot(attn_out, o_weight, preferred_element_type=jnp.f...  23.1 us
    all_gather x1, blocking collectives, shards(): dense_all = lax.all_gather(dense, 'expert', axis=0, tiled=True)  22.2 us
    dot_general x1, matrix products, shards(): gate = jnp.dot(every, w_gate[0], preferred_element_type=jnp.float32)  21.4 us
    dot_general x1, matrix products, shards(): up = jnp.dot(every, w_up[0], preferred_element_type=jnp.float32)  19.5 us
    dot_general x1, matrix products, shards(): jnp.dot(hidden, w_down[0], preferred_element_type=jnp.float32)  17.7 us
    all_gather x1, waiting for transfers between devices, shards(): lax.all_gather(mixed, 'tensor', axis=0, tiled=True)  17.2 us
  transfers between devices with their start and end apart: 4, of which 4 were waited for; matrix products, arithmetic and copies ran while one was open for 0% of the time, Pallas kernels for 0%

profile of v1, /device:TPU:0, one launch (start us, length us, event | category | flops | bytes accessed | tf_op | source)
XLA Modules:
  0.0 607.2 jit_solution(14389380256802177581)
XLA Ops:
  7.2 0.0 copy-start
  7.2 0.0 copy-start.3
  7.2 0.0 copy-start.5
  7.2 0.0 copy-start.6
  7.2 0.0 copy-start.7
  7.2 0.0 reduce-scatter.3.cloned.1.call-start
  7.3 0.9 copy-done
  8.2 9.1 %convolution_convert_fusion.1 = bf16[128,4096]{1,0:T(8,128)(2,1)} fusion(bf16[128,2048]{1,0:T(8,128)(2,1)S(1)} %copy-done, bf16[2048,4096]{1,0:T(8,128)(2,1)} %param.12), kind=kOutput, calls=%fused_computation.7 | convolution fusion | flops 2148007936 | bytes 18350080 | tf_op jit(solution)/shard_map/dot_general | solution.py:40
  17.3 0.0 reduce-scatter.3.cloned.1.call-update
  17.3 0.0 all-gather.4.cloned.1.call-start
  17.4 23.1 %reduce-scatter.3.cloned.1.call-done = bf16[64,4096]{1,0:T(8,128)(2,1)} async-done(((bf16[128,4096]{1,0:T(8,128)(2,1)}), bf16[64,4096]{1,0:T(8,128)(2,1)}) %reduce-scatter.3.cloned.1.call-update) | async-done | bytes 524304 | tf_op jit(solution)/shard_map/reduce_scatter | solution.py:39
  40.5 0.0 copy-done.3
  40.5 1.3 fusion.7
  41.8 0.0 copy-done.5
  41.8 1.0 fusion.9
  42.8 0.0 all-gather.4.cloned.1.call-update
  42.9 0.0 reduce-scatter.5.cloned.1.call-start
  42.9 0.0 copy-done.6
  42.9 0.0 copy-done.7
  43.0 22.2 %all_gather.13 = f32[2048,16]{0,1:T(8,128)S(1)} all-gather(f32[128,16]{0,1:T(8,128)S(1)} %select_reduce_fusion.1), channel_id=1, replica_groups=mesh['expert'=16,'tensor'=2] {'expert'}, dimensions={0}, use_global_device_ids=true | all-gather | bytes 139264 | tf_op jit(solution)/shard_map/all_gather | solution.py:36
  65.2 0.1 select_reduce_fusion
  65.3 94.1 %all-gather.4.cloned.1.call-done = bf16[2048,4096]{1,0:T(8,128)(2,1)} async-done(((bf16[64,4096]{1,0:T(8,128)(2,1)}), bf16[2048,4096]{1,0:T(8,128)(2,1)}) %all-gather.4.cloned.1.call-update) | async-done | bytes 16777232 | tf_op jit(solution)/shard_map/all_gather | solution.py:48
  159.4 0.0 slice-start
  159.4 19.5 %fusion.1 = f32[2048,768]{1,0:T(8,128)} fusion(bf16[2048,4096]{1,0:T(8,128)(2,1)} %all-gather.4.cloned.1.call-done, bf16[1,4096,768]{2,1,0:T(8,128)(2,1)} %param.18), kind=kOutput, calls=%fused_computation.2 | convolution fusion | flops 12884901888 | bytes 29360128 | tf_op jit(solution)/shard_map/dot_general | solution.py:51
  178.9 0.0 slice-start.1
  178.9 21.4 %multiply_convert_fusion = bf16[2048,768]{1,0:T(8,128)(2,1)} fusion(f32[2048,768]{1,0:T(8,128)} %fusion.1, bf16[2048,4096]{1,0:T(8,128)(2,1)} %all-gather.4.cloned.1.call-done, bf16[1,4096,768]{2,1,0:T(8,128)(2,1)} %param.17, f32[2048]{0:T(1024)S(1)} %select_reduce_fusion), kind=kOutput, calls=%fused_computation.6 | convolution fusion | flops 12895911936 | bytes 32514048 | tf_op jit(solution)/shard_map/dot_general | solution.py:50
  200.3 0.0 slice-done
  200.3 0.0 slice-done.1
  200.4 17.7 %convolution_convert_fusion = bf16[2048,4096]{1,0:T(8,128)(2,1)} fusion(bf16[2048,768]{1,0:T(8,128)(2,1)} %multiply_convert_fusion, bf16[1,768,4096]{2,1,0:T(8,128)(2,1)S(1)} %bitcast.23), kind=kOutput, calls=%fused_computation | convolution fusion | flops 12893290496 | bytes 26214400 | tf_op jit(solution)/shard_map/dot_general | solution.py:53
  218.1 0.0 copy-start.2
  218.1 0.0 copy-start.4
  218.1 0.0 reduce-scatter.5.cloned.1.call-update
  218.1 0.0 copy-start.1
  218.1 0.0 all-gather.6.cloned.1.call-start
  218.2 355.6 %reduce-scatter.5.cloned.1.call-done = bf16[64,4096]{1,0:T(8,128)(2,1)} async-done(((bf16[2048,4096]{1,0:T(8,128)(2,1)}), bf16[64,4096]{1,0:T(8,128)(2,1)}) %reduce-scatter.5.cloned.1.call-update) | async-done | bytes 524304 | tf_op jit(solution)/shard_map/reduce_scatter | solution.py:54
  573.8 2.0 fusion.10
  575.8 0.0 all-gather.6.cloned.1.call-update
  575.8 0.0 copy-done.2
  575.8 0.0 copy-done.4
  575.8 0.2 convolution_bitcast_fusion
  576.1 4.4 all-gather
  580.5 0.7 reshape.17
  581.1 17.2 %all-gather.6.cloned.1.call-done = bf16[128,4096]{1,0:T(8,128)(2,1)} async-done(((bf16[64,4096]{1,0:T(8,128)(2,1)}), bf16[128,4096]{1,0:T(8,128)(2,1)}) %all-gather.6.cloned.1.call-update) | async-done | bytes 1048592 | tf_op jit(solution)/shard_map/all_gather | solution.py:57
  598.4 2.3 copy.22
  600.7 0.0 copy-done.1
  (5 shorter events, 0.0 us)
Async XLA Ops:
  7.2 1.1 copy-start
  7.2 33.3 %copy-start.3 = (bf16[128,4096]{1,0:T(8,128)(2,1)S(1)}, bf16[128,4096]{1,0:T(8,128)(2,1)}, u32[]{:S(2)}) copy-start(bf16[128,4096]{1,0:T(8,128)(2,1)} %param.11) | copy-start | bytes 3145732
  7.2 34.6 %copy-start.5 = (f32[4096]{0:T(1024)S(1)}, f32[4096]{0:T(1024)}, u32[]{:S(2)}) copy-start(f32[4096]{0:T(1024)} %param.13) | copy-start | bytes 49156
  7.2 35.7 %copy-start.6 = (f32[128,8]{0,1:T(8,128)S(1)}, f32[128,8]{0,1:T(8,128)}, u32[]{:S(2)}) copy-start(f32[128,8]{0,1:T(8,128)} %param.16) | copy-start | bytes 12292
  7.2 35.7 %copy-start.7 = (s32[128,8]{0,1:T(8,128)S(1)}, s32[128,8]{0,1:T(8,128)}, u32[]{:S(2)}) copy-start(s32[128,8]{0,1:T(8,128)} %param.15) | copy-start | bytes 12292
  7.2 33.3 %reduce-scatter.3.cloned.1.call-start = ((), (), s32[]{:S(2)}) async-start(), calls=%async_computation.2 | async-start | bytes 1572864 | tf_op jit(solution)/shard_map/reduce_scatter | solution.py:39
  17.3 142.1 %all-gather.4.cloned.1.call-start = ((), (), s32[]{:S(2)}) async-start(), calls=%async_computation.3 | async-start | bytes 17301504 | tf_op jit(solution)/shard_map/all_gather | solution.py:48
  42.9 530.9 %reduce-scatter.5.cloned.1.call-start = ((), (), s32[]{:S(2)}) async-start(), calls=%async_computation.4 | async-start | bytes 17301504 | tf_op jit(solution)/shard_map/reduce_scatter | solution.py:54
  159.4 40.9 %slice-start = ((s8[6291456]{0:T(1024)(128)(4,1)}), s8[4194304]{0:T(1024)(128)(4,1)S(1)}, s32[]{:S(2)}) async-start(s8[6291456]{0:T(1024)(128)(4,1)} %bitcast.22), calls=%async_computation.6 | async-start | bytes 8388608
  178.9 21.4 %slice-start.1 = ((s8[6291456]{0:T(1024)(128)(4,1)}), s8[2097152]{0:T(1024)(128)(4,1)S(1)}, s32[]{:S(2)}) async-start(s8[6291456]{0:T(1024)(128)(4,1)} %bitcast.22), calls=%async_computation.7 | async-start | bytes 4194304
  218.1 357.7 %copy-start.2 = (bf16[64,4096]{1,0:T(8,128)(2,1)S(1)}, bf16[64,4096]{1,0:T(8,128)(2,1)}, u32[]{:S(2)}) copy-start(bf16[64,4096]{1,0:T(8,128)(2,1)} %fusion.9) | copy-start | bytes 1572868
  218.1 357.7 %copy-start.4 = (bf16[4096,16]{0,1:T(8,128)(2,1)S(1)}, bf16[4096,16]{0,1:T(8,128)(2,1)}, u32[]{:S(2)}) copy-start(bf16[4096,16]{0,1:T(8,128)(2,1)} %param.14) | copy-start | bytes 393220
  218.1 382.6 %copy-start.1 = (bf16[128,2048]{1,0:T(8,128)(2,1)S(1)}, bf16[128,2048]{1,0:T(8,128)(2,1)}, u32[]{:S(2)}) copy-start(bf16[128,2048]{1,0:T(8,128)(2,1)} %param.10) | copy-start | bytes 1572868
  218.1 380.3 %all-gather.6.cloned.1.call-start = ((), (), s32[]{:S(2)}) async-start(), calls=%async_computation.5 | async-start | bytes 1572864 | tf_op jit(solution)/shard_map/all_gather | solution.py:57
Sparse Core Ops, SparseCore 0:
  17.4 22.9 reduce-scatter.2
  44.4 115.0 all-gather.3
  218.2 355.5 reduce-scatter.4
  575.9 22.3 all-gather.5

commit v2 on v1

--- a/solution.py
+++ b/solution.py
@@ -1,9 +1,255 @@
+import functools
+
 import jax
 import jax.numpy as jnp
 from jax import lax
+from jax.experimental import pallas as pl
+from jax.experimental.pallas import tpu as pltpu
 from jax.sharding import PartitionSpec as P
 
 epsilon = 1e-06
+CUTS = 8
+
+
+class Place:
+    def __init__(self, outer):
+        e = lax.axis_index("expert")
+        self.outer = outer
+        self.y = lax.axis_index("tensor")
+        self.c = lax.rem(e, 2)
+        self.x = lax.rem(e // 2, 2)
+        self.z = e // 4
+
+    def device(self, z=None, x=None, c=None, y=None):
+        z = self.z if z is None else z
+        x = self.x if x is None else x
+        c = self.c if c is None else c
+        y = self.y if y is None else y
+        return {"expert": (z * 2 + x) * 2 + c, "tensor": y}
+
+    def far(self, j):
+        return lax.rem(self.z + j, self.outer)
+
+    def greet(self):
+        barrier = pltpu.get_barrier_semaphore()
+        peers = [self.device(c=1 - self.c), self.device(x=1 - self.x), self.device(y=1 - self.y)]
+        peers += [self.device(z=self.far(j)) for j in range(1, self.outer)]
+        for peer in peers:
+            pl.semaphore_signal(barrier, inc=1, device_id=peer, device_id_type=pl.DeviceIdType.MESH)
+        pl.semaphore_wait(barrier, len(peers))
+
+
+def remote(src, dst, send, recv, device):
+    return pltpu.make_async_remote_copy(
+        src_ref=src, dst_ref=dst, send_sem=send, recv_sem=recv,
+        device_id=device, device_id_type=pl.DeviceIdType.MESH,
+    )
+
+
+def wavefront(count, stages, lags):
+    for t in range(count + lags[-1]):
+        for stage, lag in zip(stages, lags):
+            if 0 <= t - lag < count:
+                stage(t - lag)
+
+
+def scatter_kernel(outer, h_ref, w_ref, s_ref, o_ref, acc, snd, rc, r1, r2, rz, send, recv):
+    at = Place(outer)
+    x, y, z, c = at.x, at.y, at.z, at.c
+    _, _, _, _, rows, width = acc.shape
+    block = 4 * rows
+    at.greet()
+    copies = {}
+
+    def go(k, s, src, dst, device):
+        copies[k, s] = remote(src, dst, send.at[k, s], recv.at[k, s], device)
+        copies[k, s].start()
+
+    def each(body):
+        lax.fori_loop(0, outer, lambda i, _: (body(i), 0)[1], 0)
+
+    def products(k, part, into):
+        def one(i):
+            start = pl.multiple_of(part * (outer * block) + i * block, block)
+            out = jnp.dot(
+                h_ref[pl.ds(start, block), :],
+                w_ref[:, k * width:(k + 1) * width],
+                preferred_element_type=jnp.float32,
+            )
+            into[k, i] = out.astype(jnp.bfloat16).reshape(2, 2, rows, width)
+        each(one)
+
+    def s0(k):
+        products(k, 1 - c, snd)
+        go(k, 0, snd.at[k], rc.at[k], at.device(c=1 - c))
+        products(k, c, acc)
+
+    def s1(k):
+        copies[k, 0].wait_recv()
+        if k % 2 == 0:
+            def part(v):
+                def one(i):
+                    acc[k, i, v] = acc[k, i, v] + rc[k, i, v]
+                each(one)
+            part(1 - x)
+            go(k, 1, acc.at[k, :, 1 - x], r1.at[k], at.device(x=1 - x))
+            part(x)
+        else:
+            def part(v):
+                def one(i):
+                    acc[k, i, :, v] = acc[k, i, :, v] + rc[k, i, :, v]
+                each(one)
+            part(1 - y)
+            go(k, 1, acc.at[k, :, :, 1 - y], r1.at[k], at.device(y=1 - y))
+            part(y)
+
+    def s2(k):
+        copies[k, 1].wait_recv()
+        if k % 2 == 0:
+            def part(v):
+                def one(i):
+                    acc[k, i, x, v] = acc[k, i, x, v] + r1[k, i, v]
+                each(one)
+            part(1 - y)
+            go(k, 2, acc.at[k, :, x, 1 - y], r2.at[k], at.device(y=1 - y))
+            part(y)
+        else:
+            def part(v):
+                def one(i):
+                    acc[k, i, v, y] = acc[k, i, v, y] + r1[k, i, v]
+                each(one)
+            part(1 - x)
+            go(k, 2, acc.at[k, :, 1 - x, y], r2.at[k], at.device(x=1 - x))
+            part(x)
+
+    def s3(k):
+        copies[k, 2].wait_recv()
+
+        def one(i):
+            acc[k, i, x, y] = acc[k, i, x, y] + r2[k, i]
+        each(one)
+        for j in range(1, outer):
+            d = at.far(j)
+            go(k, 3 + j, acc.at[k, d, x, y], rz.at[k, j - 1], at.device(z=d))
+
+    def s4(k):
+        cols = slice(k * width, (k + 1) * width)
+        for j in range(1, outer):
+            copies[k, 3 + j].wait_recv()
+        total = acc[k, z, x, y].astype(jnp.float32)
+        for j in range(1, outer):
+            total = total + rz[k, j - 1].astype(jnp.float32)
+        o_ref[y, :, cols] = (s_ref[:, cols].astype(jnp.float32) + total).astype(jnp.bfloat16)
+        go(k, 3, o_ref.at[y, :, cols], o_ref.at[y, :, cols], at.device(y=1 - y))
+
+    wavefront(CUTS, [s0, s1, s2, s3, s4], [0, 1, 3, 5, 7])
+    for k in range(CUTS):
+        copies[k, 3].wait_recv()
+    for copy in copies.values():
+        copy.wait_send()
+
+
+def experts_home(hidden, w_down, stream, outer):
+    rows, width = stream.shape
+    cut = width // CUTS
+    vmem = pl.BlockSpec(memory_space=pltpu.VMEM)
+    bf16 = jnp.bfloat16
+    return pl.pallas_call(
+        functools.partial(scatter_kernel, outer),
+        out_shape=jax.ShapeDtypeStruct((2, rows, width), bf16),
+        in_specs=[vmem] * 3,
+        out_specs=vmem,
+        scratch_shapes=[
+            pltpu.VMEM((CUTS, outer, 2, 2, rows, cut), bf16),
+            pltpu.VMEM((CUTS, outer, 2, 2, rows, cut), bf16),
+            pltpu.VMEM((CUTS, outer, 2, 2, rows, cut), bf16),
+            pltpu.VMEM((CUTS, outer, 2, rows, cut), bf16),
+            pltpu.VMEM((CUTS, outer, rows, cut), bf16),
+            pltpu.VMEM((CUTS, outer - 1, rows, cut), bf16),
+            pltpu.SemaphoreType.DMA((CUTS, outer + 3)),
+            pltpu.SemaphoreType.DMA((CUTS, outer + 3)),
+        ],
+        compiler_params=pltpu.CompilerParams(
+            collective_id=1, has_side_effects=True, vmem_limit_bytes=56 << 20
+        ),
+    )(hidden, w_down, stream)
+
+
+def gather_kernel(outer, n_ref, e_ref, o_ref, eo_ref, send, recv, local):
+    at = Place(outer)
+    x, y, z, c = at.x, at.y, at.z, at.c
+    width = n_ref.shape[1] // CUTS
+    own = [
+        pltpu.make_async_copy(n_ref, o_ref.at[c, z, x, y], local.at[0]),
+        pltpu.make_async_copy(e_ref, eo_ref.at[c, z, x, y], local.at[1]),
+    ]
+    for copy in own:
+        copy.start()
+    at.greet()
+    copies = {}
+
+    def go(k, s, src, dst, device):
+        copies[k, s] = remote(src, dst, send.at[k, s], recv.at[k, s], device)
+        copies[k, s].start()
+
+    def refs(k):
+        if k == 0:
+            return e_ref, eo_ref, slice(None)
+        return n_ref, o_ref, pl.ds((k - 1) * width, width)
+
+    for k in range(CUTS + 1):
+        src, dst, cols = refs(k)
+        for j in range(1, outer):
+            go(k, 2 + j, src.at[:, cols], dst.at[c, z, x, y, :, cols], at.device(z=at.far(j)))
+    for copy in own:
+        copy.wait()
+
+    def s1(k):
+        for j in range(1, outer):
+            copies[k, 2 + j].wait_recv()
+        _, ref, cols = refs(k)
+        part = ref.at[c, :, x, y, :, cols]
+        go(k, 0, part, part, at.device(x=1 - x) if k % 2 else at.device(y=1 - y))
+
+    def s2(k):
+        copies[k, 0].wait_recv()
+        _, ref, cols = refs(k)
+        if k % 2:
+            part = ref.at[c, :, :, y, :, cols]
+            go(k, 1, part, part, at.device(y=1 - y))
+        else:
+            part = ref.at[c, :, x, :, :, cols]
+            go(k, 1, part, part, at.device(x=1 - x))
+
+    def s3(k):
+        copies[k, 1].wait_recv()
+        _, ref, cols = refs(k)
+        part = ref.at[c, :, :, :, :, cols]
+        go(k, 2, part, part, at.device(c=1 - c))
+
+    wavefront(CUTS + 1, [s1, s2, s3], [0, 2, 4])
+    for k in range(CUTS + 1):
+        copies[k, 2].wait_recv()
+    for copy in copies.values():
+        copy.wait_send()
+
+
+def gather_rows(normed, extra, outer):
+    anywhere = pl.BlockSpec(memory_space=pl.ANY)
+    return pl.pallas_call(
+        functools.partial(gather_kernel, outer),
+        out_shape=[
+            jax.ShapeDtypeStruct((2, outer, 2, 2, *v.shape), v.dtype) for v in (normed, extra)
+        ],
+        in_specs=[anywhere] * 2,
+        out_specs=[anywhere] * 2,
+        scratch_shapes=[
+            pltpu.SemaphoreType.DMA((CUTS + 1, outer + 2)),
+            pltpu.SemaphoreType.DMA((CUTS + 1, outer + 2)),
+            pltpu.SemaphoreType.DMA((2,)),
+        ],
+        compiler_params=pltpu.CompilerParams(collective_id=2, has_side_effects=True),
+    )(normed, extra)
 
 
 def rms_scaled(stream, norm_gain):
@@ -58,6 +304,56 @@
         lax.all_gather(logits, "tensor", axis=0, tiled=True),
     )
 
+def shards_paired(
+    attn_out,
+    residual,
+    o_weight,
+    norm_gain,
+    router_weight,
+    expert_idx,
+    combine,
+    w_gate,
+    w_up,
+    w_down,
+):
+    y = lax.axis_index("tensor")
+    me = lax.axis_index("expert")
+    outer = lax.axis_size("expert") // 4
+    rows = residual.shape[0] // 2
+    width = residual.shape[1]
+    expert_count = router_weight.shape[1]
+    bf16 = jnp.bfloat16
+
+    def take(array, at):
+        return lax.dynamic_slice_in_dim(array, at * rows, rows, 0)
+
+    experts = jnp.arange(expert_count, dtype=jnp.int32)
+    dense = jnp.sum(
+        jnp.where(take(expert_idx, y)[:, :, None] == experts, take(combine, y)[:, :, None], 0.0),
+        axis=1,
+    )
+    high = dense.astype(bf16)
+    low = (dense - high.astype(jnp.float32)).astype(bf16)
+    extra = jnp.pad(jnp.concatenate([high, low], axis=1), ((0, 0), (0, -2 * expert_count % 128)))
+
+    partial = jnp.dot(attn_out, o_weight, preferred_element_type=jnp.float32).astype(bf16)
+    came = lax.ppermute(take(partial, 1 - y), "tensor", [(0, 1), (1, 0)])
+    projected = take(partial, y).astype(jnp.float32) + came.astype(jnp.float32)
+    stream = (take(residual, y).astype(jnp.float32) + projected).astype(bf16)
+    normed = rms_scaled(stream, norm_gain)
+    every, extras = gather_rows(normed, extra, outer)
+    group = every[me % 2, me // 4, (me // 2) % 2].reshape(2 * rows, width)
+    logits = jnp.dot(group, router_weight, preferred_element_type=jnp.float32)
+    every = every.reshape(-1, width)
+    extras = extras.reshape(-1, extra.shape[1]).astype(jnp.float32)
+    named = extras[:, :expert_count] + extras[:, expert_count:2 * expert_count]
+    mine = jnp.sum(jnp.where(experts == me, named, 0.0), axis=1, keepdims=True)
+    gate = jnp.dot(every, w_gate[0], preferred_element_type=jnp.float32)
+    up = jnp.dot(every, w_up[0], preferred_element_type=jnp.float32)
+    hidden = (jax.nn.silu(gate) * up * mine).astype(bf16)
+    mixed = experts_home(hidden, w_down[0], stream, outer)
+    return mixed.reshape(2 * rows, width), logits
+
 
 def solution(mesh):
     in_specs = (
@@ -73,4 +369,7 @@
         P("expert", "tensor", None),
     )
     out_specs = (P("expert", None), P("expert", None))
-    return jax.shard_map(shards, mesh=mesh, in_specs=in_specs, out_specs=out_specs, check_vma=False)
+    paired = mesh.shape["tensor"] == 2 and mesh.shape["expert"] % 4 == 0
+    paired = paired and mesh.shape["expert"] > 4
+    body = shards_paired if paired else shards
+    return jax.shard_map(body, mesh=mesh, in_specs=in_specs, out_specs=out_specs, check_vma=False)

time: 608 us -> 275 us (0.45)
  waiting for transfers between devices: 490 us -> 10.8 us
  Pallas kernels: 0 us -> 205 us
  blocking collectives: 26.6 us -> 0 us
  matrix products: 68 us -> 45.8 us
  between operations: 13.9 us -> 0.83 us
    reduce_scatter x2 -> x0, waiting for transfers between devices: 379 us -> none  [the longest x1 356 us: shards(): lax.psum_scatter(part, ('expert', 'tensor'), scatter_dimension=0, tiled=T...]
    pallas_call x0 -> x2, Pallas kernels: none -> 205 us  [the longest x1 109 us: experts_home(): pl.pallas_call(functools.partial(scatter_kernel, outer), out_shape=jax.Sh...]
    all_gather x2 -> x0, waiting for transfers between devices: 111 us -> none  [the longest x1 94.1 us: shards(): every = lax.all_gather(normed, ('expert', 'tensor'), axis=0, tiled=True)]
    all_gather x2 -> x0, blocking collectives: 26.6 us -> none  [the longest x1 22.2 us: shards(): dense_all = lax.all_gather(dense, 'expert', axis=0, tiled=True)]
    dot_general x5 -> x4, matrix products: 68 us -> 45.8 us  [the longest x1 18.6 us: shards_paired(): up = jnp.dot(every, w_up[0], preferred_element_type=jnp.float32)]
    ppermute x0 -> x1, waiting for transfers between devices: none -> 10.8 us  [shards_paired(): came = lax.ppermute(take(partial, 1 - y), 'tensor', [(0, 1), (1, 0)])]
  transfers between devices with their start and end apart: 4 -> 1, of which waited for: 4 -> 1; matrix products, arithmetic and copies ran while one was open for 0% -> 0% of each run, Pallas kernels for 0% -> 0%
where the time goes in v2:
time: 275 us
  Pallas kernels  205 us (75%)
  matrix products  45.8 us (17%)
  waiting for transfers between devices  10.8 us (4%)
  local copies, waits for them, and re-layouts  5.04 us (2%)
  other arithmetic  3.96 us (1%)
  starting transfers between devices  3.03 us (1%)
    pallas_call x1, Pallas kernels, experts_home(): pl.pallas_call(functools.partial(scatter_kernel, outer), out_shape=jax.Sh...  109 us
    pallas_call x1, Pallas kernels, gather_rows(): pl.pallas_call(functools.partial(gather_kernel, outer), out_shape=[jax.Sh...  95.9 us
    dot_general x1, matrix products, shards_paired(): up = jnp.dot(every, w_up[0], preferred_element_type=jnp.float32)  18.6 us
    dot_general x1, matrix products, shards_paired(): gate = jnp.dot(every, w_gate[0], preferred_element_type=jnp.float32)  18.1 us
    ppermute x1, waiting for transfers between devices, shards_paired(): came = lax.ppermute(take(partial, 1 - y), 'tensor', [(0, 1), (1, 0)])  10.8 us
    dot_general x1, matrix products, shards_paired(): jnp.dot(attn_out, o_weight, preferred_element_type=jnp.float32).astype(bf16)  8.2 us
  transfers between devices with their start and end apart: 1, of which 1 were waited for; matrix products, arithmetic and copies ran while one was open for 0% of the time, Pallas kernels for 0%

profile of v2, /device:TPU:0, one launch (start us, length us, event | category | flops | bytes accessed | tf_op | source)
XLA Modules:
  0.0 274.5 jit_solution(18260782606143150186)
XLA Ops:
  0.6 0.0 copy-start
  0.7 1.0 copy-done
  1.7 0.0 copy-start.6
  1.7 0.0 copy-start.7
  1.7 0.0 copy-start.3
  1.7 0.0 copy-start.5
  1.7 8.2 %convolution_convert_fusion = bf16[128,4096]{1,0:T(8,128)(2,1)S(1)} fusion(bf16[128,2048]{1,0:T(8,128)(2,1)S(1)} %copy-done, bf16[2048,4096]{1,0:T(8,128)(2,1)} %param.12), kind=kOutput, calls=%fused_computation.5 | convolution fusion | flops 2148007936 | bytes 18350080 | tf_op jit(solution)/shard_map/dot_general | solution.py:339
  10.0 3.0 %collective-permute-start = (bf16[64,4096]{1,0:T(8,128)(2,1)S(1)}, bf16[64,4096]{1,0:T(8,128)(2,1)S(1)}, u32[]{:S(2)}, u32[]{:S(2)}) collective-permute-start(bf16[64,4096]{1,0:T(8,128)(2,1)S(1)} %constant_dynamic-slice_fusion.2), channel_id=1, source_target_pairs={{0,1},{1,0},{2,3},{3,2},{4,5},{5,4},{6,7},{7,6},{8,9},{9,8},{10,11... | collective-permute-start | bytes 1572872 | tf_op jit(solution)/shard_map/ppermute | solution.py:340
  13.0 0.0 copy-done.6
  13.0 0.1 constant_dynamic-slice_fusion
  13.1 0.0 copy-done.7
  13.1 0.1 constant_dynamic-slice_fusion.1
  13.2 0.1 copy.17
  13.3 0.1 copy.18
  13.4 0.7 fusion.13.e_ref
  14.1 10.8 %collective-permute-done = bf16[64,4096]{1,0:T(8,128)(2,1)S(1)} collective-permute-done((bf16[64,4096]{1,0:T(8,128)(2,1)S(1)}, bf16[64,4096]{1,0:T(8,128)(2,1)S(1)}, u32[]{:S(2)}, u32[]{:S(2)}) %collective-permute-start) | collective-permute-done | bytes 524320 | tf_op jit(solution)/shard_map/ppermute | solution.py:340
  24.9 0.0 copy-done.3
  24.9 0.4 fusion.6
  25.3 0.0 copy-start.2
  25.3 0.0 copy-done.5
  25.3 1.0 fusion.8.n_ref
  26.3 95.9 %shard_map.113 = (bf16[2,4,2,2,64,4096]{5,4,3,2,1,0:T(8,128)(2,1)}, bf16[2,4,2,2,64,128]{5,4,3,2,1,0:T(8,128)(2,1)}) custom-call(bf16[64,4096]{1,0:T(8,128)(2,1)} %fusion.8.n_ref, bf16[64,128]{1,0:T(8,128)(2,1)} %fusion.13.e_ref), custom_call_target="tpu_custom_call" | custom-call | tf_op jit(solution)/shard_map/pallas_call | solution.py:239
  122.2 0.0 slice-start
  122.2 1.3 convert.1
  123.5 0.0 slice-start.1
  123.5 18.6 %fusion = f32[2048,768]{1,0:T(8,128)S(1)} fusion(bf16[2048,4096]{1,0:T(8,128)(2,1)} %bitcast.24, bf16[1,4096,768]{2,1,0:T(8,128)(2,1)} %param.18), kind=kOutput, calls=%fused_computation | convolution fusion | flops 12884901888 | bytes 29360128 | tf_op jit(solution)/shard_map/dot_general | solution.py:352
  142.1 0.0 copy-done.2
  142.1 0.6 fusion.10
  142.7 0.0 slice-done
  142.7 0.0 slice-done.1
  142.8 18.1 %multiply_convert_fusion.h_ref = bf16[2048,768]{1,0:T(8,128)(2,1)} fusion(f32[2048,768]{1,0:T(8,128)S(1)} %fusion, bf16[2048,4096]{1,0:T(8,128)(2,1)} %bitcast.25, bf16[1,4096,768]{2,1,0:T(8,128)(2,1)S(1)} %bitcast.27, f32[2048]{0:T(1024)S(1)} %fusion.10), kind=kOutput, calls=%fused_computation.4 | convolution fusion | flops 12895911936 | bytes 32514048 | tf_op jit(solution)/shard_map/dot_general | solution.py:351
  160.8 0.0 copy-start.1
  160.8 0.0 copy-start.4
  160.8 109.1 %shard_map.114 = bf16[2,64,4096]{2,1,0:T(8,128)(2,1)} custom-call(bf16[2048,768]{1,0:T(8,128)(2,1)} %multiply_convert_fusion.h_ref, bf16[768,4096]{1,0:T(8,128)(2,1)} %bitcast.20, bf16[64,4096]{1,0:T(8,128)(2,1)} %copy-done.2), custom_call_target="tpu_custom_call" | custom-call | tf_op jit(solution)/shard_map/pallas_call | solution.py:157
  269.9 1.3 constant_dynamic-slice_fusion.3
  271.2 0.0 copy-done.4
  271.2 1.0 fusion.14
  272.2 2.3 copy.20
  274.5 0.0 copy-done.1
  (7 shorter events, 0.1 us)
Async XLA Ops:
  0.6 1.1 copy-start
  1.7 11.3 %copy-start.6 = (f32[128,8]{0,1:T(8,128)S(1)}, f32[128,8]{0,1:T(8,128)}, u32[]{:S(2)}) copy-start(f32[128,8]{0,1:T(8,128)} %param.16) | copy-start | bytes 12292
  1.7 11.4 %copy-start.7 = (s32[128,8]{0,1:T(8,128)S(1)}, s32[128,8]{0,1:T(8,128)}, u32[]{:S(2)}) copy-start(s32[128,8]{0,1:T(8,128)} %param.15) | copy-start | bytes 12292
  1.7 23.2 %copy-start.3 = (bf16[128,4096]{1,0:T(8,128)(2,1)S(1)}, bf16[128,4096]{1,0:T(8,128)(2,1)}, u32[]{:S(2)}) copy-start(bf16[128,4096]{1,0:T(8,128)(2,1)} %param.11) | copy-start | bytes 3145732
  1.7 23.6 %copy-start.5 = (f32[4096]{0:T(1024)S(1)}, f32[4096]{0:T(1024)}, u32[]{:S(2)}) copy-start(f32[4096]{0:T(1024)} %param.13) | copy-start | bytes 49156
  10.0 15.0 %collective-permute-start = (bf16[64,4096]{1,0:T(8,128)(2,1)S(1)}, bf16[64,4096]{1,0:T(8,128)(2,1)S(1)}, u32[]{:S(2)}, u32[]{:S(2)}) collective-permute-start(bf16[64,4096]{1,0:T(8,128)(2,1)S(1)} %constant_dynamic-slice_fusion.2), channel_id=1, source_target_pairs={{0,1},{1,0},{2,3},{3,2},{4,5},{5,4},{6,7},{7,6},{8,9},{9,8},{10,11... | collective-permute-start | bytes 1572872 | tf_op jit(solution)/shard_map/ppermute | solution.py:340
  25.3 116.8 %copy-start.2 = (bf16[64,4096]{1,0:T(8,128)(2,1)}, bf16[64,4096]{1,0:T(8,128)(2,1)S(1)}, u32[]{:S(2)}) copy-start(bf16[64,4096]{1,0:T(8,128)(2,1)S(1)} %get-tuple-element.7.s_ref) | copy-start | bytes 1572868
  122.2 20.5 %slice-start = ((s8[6291456]{0:T(1024)(128)(4,1)}), s8[4194304]{0:T(1024)(128)(4,1)S(1)}, s32[]{:S(2)}) async-start(s8[6291456]{0:T(1024)(128)(4,1)} %bitcast.26), calls=%async_computation | async-start | bytes 8388608
  123.5 19.3 %slice-start.1 = ((s8[6291456]{0:T(1024)(128)(4,1)}), s8[2097152]{0:T(1024)(128)(4,1)S(1)}, s32[]{:S(2)}) async-start(s8[6291456]{0:T(1024)(128)(4,1)} %bitcast.26), calls=%async_computation.1 | async-start | bytes 4194304
  160.8 113.7 %copy-start.1 = (bf16[128,2048]{1,0:T(8,128)(2,1)S(1)}, bf16[128,2048]{1,0:T(8,128)(2,1)}, u32[]{:S(2)}) copy-start(bf16[128,2048]{1,0:T(8,128)(2,1)} %param.10) | copy-start | bytes 1572868
  160.8 110.4 %copy-start.4 = (bf16[4096,16]{0,1:T(8,128)(2,1)S(1)}, bf16[4096,16]{0,1:T(8,128)(2,1)}, u32[]{:S(2)}) copy-start(bf16[4096,16]{0,1:T(8,128)(2,1)} %param.14) | copy-start | bytes 393220

commit v3 on v2

--- a/solution.py
+++ b/solution.py
@@ -175,81 +175,133 @@
     )(hidden, w_down, stream)
 
 
-def gather_kernel(outer, n_ref, e_ref, o_ref, eo_ref, send, recv, local):
+def gather_kernel(
+    outer, n_ref, e_ref, g_hbm, u_hbm, r_ref, h_ref, l_ref,
+    every, extras, g_ref, u_ref, gate, up, send, recv, local,
+):
     at = Place(outer)
     x, y, z, c = at.x, at.y, at.z, at.c
+    me = lax.axis_index("expert")
+    rows = n_ref.shape[0]
     width = n_ref.shape[1] // CUTS
-    own = [
-        pltpu.make_async_copy(n_ref, o_ref.at[c, z, x, y], local.at[0]),
-        pltpu.make_async_copy(e_ref, eo_ref.at[c, z, x, y], local.at[1]),
+    count = r_ref.shape[1]
+    block = 4 * rows
+    weights = [
+        pltpu.make_async_copy(g_hbm, g_ref, local.at[0]),
+        pltpu.make_async_copy(u_hbm, u_ref, local.at[1]),
     ]
-    for copy in own:
+    for copy in weights:
         copy.start()
+    extras[c, z, x, y] = e_ref[...]
+    for k in range(CUTS):
+        every[k, c, z, x, y] = n_ref[:, k * width:(k + 1) * width]
+    l_ref[...] = jnp.zeros_like(l_ref)
     at.greet()
     copies = {}
 
-    def go(k, s, src, dst, device):
-        copies[k, s] = remote(src, dst, send.at[k, s], recv.at[k, s], device)
+    def go(k, s, part, device):
+        copies[k, s] = remote(part, part, send.at[k, s], recv.at[k, s], device)
         copies[k, s].start()
 
-    def refs(k):
-        if k == 0:
-            return e_ref, eo_ref, slice(None)
-        return n_ref, o_ref, pl.ds((k - 1) * width, width)
-
-    for k in range(CUTS + 1):
-        src, dst, cols = refs(k)
+    def held(k):
+        return extras if k == 0 else every.at[k - 1]
+
+    def compute(k, half):
+        cols = slice((k - 1) * width, k * width)
+
+        def one(i, _):
+            lhs = every[k - 1, half, i].reshape(block, width)
+            g = jnp.dot(lhs, g_ref[cols, :], preferred_element_type=jnp.float32)
+            u = jnp.dot(lhs, u_ref[cols, :], preferred_element_type=jnp.float32)
+            if k > 1:
+                g = g + gate[half, i]
+                u = u + up[half, i]
+            if k < CUTS:
+                gate[half, i] = g
+                up[half, i] = u
+            else:
+                pair = extras[half, i].reshape(block, -1).astype(jnp.float32)
+                lane = lax.broadcasted_iota(jnp.int32, pair.shape, 1)
+                chosen = (lane == me) | (lane == me + count)
+                mine = jnp.sum(jnp.where(chosen, pair, 0.0), axis=1, keepdims=True)
+                value = g / (1.0 + jnp.exp(-g)) * u * mine
+                start = pl.multiple_of((half * outer + i) * block, block)
+                h_ref[pl.ds(start, block), :] = value.astype(jnp.bfloat16)
+            return 0
+
+        lax.fori_loop(0, outer, one, 0)
+
+    def s0(k):
         for j in range(1, outer):
-            go(k, 2 + j, src.at[:, cols], dst.at[c, z, x, y, :, cols], at.device(z=at.far(j)))
-    for copy in own:
-        copy.wait()
+            go(k, 2 + j, held(k).at[c, z, x, y], at.device(z=at.far(j)))
 
     def s1(k):
         for j in range(1, outer):
             copies[k, 2 + j].wait_recv()
-        _, ref, cols = refs(k)
-        part = ref.at[c, :, x, y, :, cols]
-        go(k, 0, part, part, at.device(x=1 - x) if k % 2 else at.device(y=1 - y))
+        go(k, 0, held(k).at[c, :, x, y], at.device(x=1 - x) if k % 2 else at.device(y=1 - y))
 
     def s2(k):
         copies[k, 0].wait_recv()
-        _, ref, cols = refs(k)
         if k % 2:
-            part = ref.at[c, :, :, y, :, cols]
-            go(k, 1, part, part, at.device(y=1 - y))
+            go(k, 1, held(k).at[c, :, :, y], at.device(y=1 - y))
         else:
-            part = ref.at[c, :, x, :, :, cols]
-            go(k, 1, part, part, at.device(x=1 - x))
+            go(k, 1, held(k).at[c, :, x], at.device(x=1 - x))
 
     def s3(k):
         copies[k, 1].wait_recv()
-        _, ref, cols = refs(k)
-        part = ref.at[c, :, :, :, :, cols]
-        go(k, 2, part, part, at.device(c=1 - c))
-
-    wavefront(CUTS + 1, [s1, s2, s3], [0, 2, 4])
-    for k in range(CUTS + 1):
+        go(k, 2, held(k).at[c], at.device(c=1 - c))
+        if k == 1:
+            for copy in weights:
+                copy.wait()
+        if 0 < k < CUTS:
+            compute(k, c)
+
+    def s4(k):
+        if k == CUTS:
+            compute(k, c)
+        if k > 0:
+            group = every[k - 1, c, z, x].reshape(2 * rows, width)
+            router = r_ref[(k - 1) * width:k * width, :]
+            l_ref[...] += jnp.dot(group, router, preferred_element_type=jnp.float32)
         copies[k, 2].wait_recv()
+        if k > 0:
+            compute(k, 1 - c)
+
+    wavefront(CUTS + 1, [s0, s1, s2, s3, s4], [0, 2, 4, 6, 7])
     for copy in copies.values():
         copy.wait_send()
 
 
-def gather_rows(normed, extra, outer):
+def gather_hidden(normed, extra, w_gate, w_up, router, outer):
+    rows, width = normed.shape
+    cut = width // CUTS
+    units = w_gate.shape[1]
+    bf16, f32 = jnp.bfloat16, jnp.float32
+    vmem = pl.BlockSpec(memory_space=pltpu.VMEM)
     anywhere = pl.BlockSpec(memory_space=pl.ANY)
     return pl.pallas_call(
         functools.partial(gather_kernel, outer),
         out_shape=[
-            jax.ShapeDtypeStruct((2, outer, 2, 2, *v.shape), v.dtype) for v in (normed, extra)
+            jax.ShapeDtypeStruct((8 * outer * rows, units), bf16),
+            jax.ShapeDtypeStruct((2 * rows, router.shape[1]), f32),
         ],
-        in_specs=[anywhere] * 2,
-        out_specs=[anywhere] * 2,
+        in_specs=[vmem, vmem, anywhere, anywhere, vmem],
+        out_specs=[vmem] * 2,
         scratch_shapes=[
+            pltpu.VMEM((CUTS, 2, outer, 2, 2, rows, cut), bf16),
+            pltpu.VMEM((2, outer, 2, 2, *extra.shape), bf16),
+            pltpu.VMEM((width, units), bf16),
+            pltpu.VMEM((width, units), bf16),
+            pltpu.VMEM((2, outer, 4 * rows, units), f32),
+            pltpu.VMEM((2, outer, 4 * rows, units), f32),
             pltpu.SemaphoreType.DMA((CUTS + 1, outer + 2)),
             pltpu.SemaphoreType.DMA((CUTS + 1, outer + 2)),
             pltpu.SemaphoreType.DMA((2,)),
         ],
-        compiler_params=pltpu.CompilerParams(collective_id=2, has_side_effects=True),
-    )(normed, extra)
+        compiler_params=pltpu.CompilerParams(
+            collective_id=2, has_side_effects=True, vmem_limit_bytes=58 << 20
+        ),
+    )(normed, extra, w_gate, w_up, router)
 
 
 def rms_scaled(stream, norm_gain):
@@ -336,21 +388,18 @@
     low = (dense - high.astype(jnp.float32)).astype(bf16)
     extra = jnp.pad(jnp.concatenate([high, low], axis=1), ((0, 0), (0, -2 * expert_count % 128)))
 
-    partial = jnp.dot(attn_out, o_weight, preferred_element_type=jnp.float32).astype(bf16)
-    came = lax.ppermute(take(partial, 1 - y), "tensor", [(0, 1), (1, 0)])
-    projected = take(partial, y).astype(jnp.float32) + came.astype(jnp.float32)
+    pieces = []
+    cut = width // 4
+    for i in range(4):
+        partial = jnp.dot(
+            attn_out, o_weight[:, i * cut:(i + 1) * cut], preferred_element_type=jnp.float32
+        ).astype(bf16)
+        came = lax.ppermute(take(partial, 1 - y), "tensor", [(0, 1), (1, 0)])
+        pieces.append(take(partial, y).astype(jnp.float32) + came.astype(jnp.float32))
+    projected = jnp.concatenate(pieces, axis=1)
     stream = (take(residual, y).astype(jnp.float32) + projected).astype(bf16)
     normed = rms_scaled(stream, norm_gain)
-    every, extras = gather_rows(normed, extra, outer)
-    group = every[me % 2, me // 4, (me // 2) % 2].reshape(2 * rows, width)
-    logits = jnp.dot(group, router_weight, preferred_element_type=jnp.float32)
-    every = every.reshape(-1, width)
-    extras = extras.reshape(-1, extra.shape[1]).astype(jnp.float32)
-    named = extras[:, :expert_count] + extras[:, expert_count:2 * expert_count]
-    mine = jnp.sum(jnp.where(experts == me, named, 0.0), axis=1, keepdims=True)
-    gate = jnp.dot(every, w_gate[0], preferred_element_type=jnp.float32)
-    up = jnp.dot(every, w_up[0], preferred_element_type=jnp.float32)
-    hidden = (jax.nn.silu(gate) * up * mine).astype(bf16)
+    hidden, logits = gather_hidden(normed, extra, w_gate[0], w_up[0], router_weight, outer)
     mixed = experts_home(hidden, w_down[0], stream, outer)
     return mixed.reshape(2 * rows, width), logits
 

time: 275 us -> 239 us (0.87)
  matrix products: 45.8 us -> 11.7 us
  waiting for transfers between devices: 10.8 us -> 2.39 us
  Pallas kernels: 205 us -> 209 us
    dot_general x4, matrix products: 45.8 us -> 11.7 us  [shards_paired(): jnp.dot(attn_out, o_weight[:, i * cut:(i + 1) * cut], preferred_element_t...]
    ppermute x1 -> x4, waiting for transfers between devices: 10.8 us -> 2.39 us  [shards_paired(): came = lax.ppermute(take(partial, 1 - y), 'tensor', [(0, 1), (1, 0)])]
    pallas_call x1, Pallas kernels: 95.9 us -> 104 us  [gather_hidden(): pl.pallas_call(functools.partial(gather_kernel, outer), out_shape=[jax.Sh...]
    pallas_call x1, Pallas kernels: 109 us -> 105 us  [experts_home(): pl.pallas_call(functools.partial(scatter_kernel, outer), out_shape=jax.Sh...]
  transfers between devices with their start and end apart: 1 -> 4, of which waited for: 1 -> 1; matrix products, arithmetic and copies ran while one was open for 0% -> 5% of each run, Pallas kernels for 0% -> 0%
where the time goes in v3:
time: 239 us
  Pallas kernels  209 us (87%)
  matrix products  11.7 us (5%)
  local copies, waits for them, and re-layouts  7.68 us (3%)
  starting transfers between devices  5.06 us (2%)
  waiting for transfers between devices  2.39 us (1%)
    pallas_call x1, Pallas kernels, experts_home(): pl.pallas_call(functools.partial(scatter_kernel, outer), out_shape=jax.Sh...  105 us
    pallas_call x1, Pallas kernels, gather_hidden(): pl.pallas_call(functools.partial(gather_kernel, outer), out_shape=[jax.Sh...  104 us
    dot_general x4, matrix products, shards_paired(): jnp.dot(attn_out, o_weight[:, i * cut:(i + 1) * cut], preferred_element_t...  11.7 us
    unnamed x19, local copies, waits for them, and re-layouts  5.34 us
    ppermute x4, starting transfers between devices, shards_paired(): came = lax.ppermute(take(partial, 1 - y), 'tensor', [(0, 1), (1, 0)])  5.06 us
  transfers between devices with their start and end apart: 4, of which 1 were waited for; matrix products, arithmetic and copies ran while one was open for 5% of the time, Pallas kernels for 0%

profile of v3, /device:TPU:0, one launch (start us, length us, event | category | flops | bytes accessed | tf_op | source)
XLA Modules:
  0.0 238.6 jit_solution(726241424098236058)
XLA Ops:
  0.6 0.0 copy-start
  0.7 1.0 copy-done
  1.7 2.9 %fusion.11 = bf16[128,1024]{1,0:T(8,128)(2,1)S(1)} fusion(bf16[128,2048]{1,0:T(8,128)(2,1)S(1)} %copy-done, bf16[2048,4096]{1,0:T(8,128)(2,1)} %param.12), kind=kOutput, calls=%fused_computation.11 | convolution fusion | flops 537001984 | bytes 4980736 | tf_op jit(solution)/shard_map/dot_general | solution.py:394
  4.6 0.7 constant_dynamic-slice_fusion.4
  5.3 3.0 %collective-permute-start.1 = (bf16[64,1024]{1,0:T(8,128)(2,1)}, bf16[64,1024]{1,0:T(8,128)(2,1)S(1)}, u32[]{:S(2)}, u32[]{:S(2)}) collective-permute-start(bf16[64,1024]{1,0:T(8,128)(2,1)} %constant_dynamic-slice_fusion.4), channel_id=1, source_target_pairs={{0,1},{1,0},{2,3},{3,2},{4,5},{5,4},{6,7},{7,6},{8,9},{9,8},{10,11... | collective-permute-start | bytes 393224 | tf_op jit(solution)/shard_map/ppermute | solution.py:397
  8.2 2.9 %fusion.8 = bf16[128,1024]{1,0:T(8,128)(2,1)S(1)} fusion(bf16[128,2048]{1,0:T(8,128)(2,1)S(1)} %copy-done, bf16[2048,4096]{1,0:T(8,128)(2,1)} %param.12), kind=kOutput, calls=%fused_computation.10 | convolution fusion | flops 537001984 | bytes 4980736 | tf_op jit(solution)/shard_map/dot_general | solution.py:394
  11.1 0.7 constant_dynamic-slice_fusion.5
  11.8 0.0 copy-start.6
  11.8 0.0 copy-start.7
  11.8 0.0 copy-start.3
  11.8 0.0 collective-permute-start
  11.8 3.0 %fusion.17 = bf16[128,1024]{1,0:T(8,128)(2,1)S(1)} fusion(bf16[128,2048]{1,0:T(8,128)(2,1)S(1)} %copy-done, bf16[2048,4096]{1,0:T(8,128)(2,1)} %param.12), kind=kOutput, calls=%fused_computation.13 | convolution fusion | flops 537001984 | bytes 4980736 | tf_op jit(solution)/shard_map/dot_general | solution.py:394
  14.8 0.0 copy-start.2
  14.8 0.0 copy-start.5
  14.8 0.7 constant_dynamic-slice_fusion.2
  15.5 2.0 collective-permute-start.3
  17.4 2.9 %fusion.14 = bf16[128,1024]{1,0:T(8,128)(2,1)S(1)} fusion(bf16[128,2048]{1,0:T(8,128)(2,1)S(1)} %copy-done, bf16[2048,4096]{1,0:T(8,128)(2,1)} %param.12), kind=kOutput, calls=%fused_computation.12 | convolution fusion | flops 537001984 | bytes 4980736 | tf_op jit(solution)/shard_map/dot_general | solution.py:394
  20.4 0.1 collective-permute-start.2
  20.5 0.0 copy-done.6
  20.5 0.1 constant_dynamic-slice_fusion.1
  20.6 0.0 copy-done.7
  20.6 0.1 constant_dynamic-slice_fusion
  20.7 0.1 copy.21
  20.8 0.1 copy.22
  20.9 0.0 copy-done.3
  20.9 1.3 copy.23.r_ref
  22.2 0.7 fusion.26.e_ref
  22.9 0.0 collective-permute-done.1
  22.9 0.0 collective-permute-done
  23.0 0.0 collective-permute-done.3
  23.0 2.4 collective-permute-done.2
  25.4 0.0 copy-done.2
  25.4 0.3 fusion.20
  25.7 0.0 copy-start.1
  25.7 0.0 copy-done.5
  25.7 1.0 fusion.22.n_ref
  26.7 103.8 %shard_map.113 = (bf16[2048,768]{1,0:T(8,128)(2,1)}, f32[128,16]{1,0:T(8,128)}) custom-call(bf16[64,4096]{1,0:T(8,128)(2,1)} %fusion.22.n_ref, bf16[64,128]{1,0:T(8,128)(2,1)} %fusion.26.e_ref, bf16[4096,768]{1,0:T(8,128)(2,1)} %bitcast.8, bf16[4096,768]{1,0:T(8,128)(2,1)} %bitcast.9, bf16[4096,16]{1,0:T(8,128)(2,1)} %copy.23.r_ref), custom_call_target="tpu_custom_call" | custom-call | tf_op jit(solution)/shard_map/pallas_call | solution.py:282
  130.5 0.0 copy-done.1
  130.5 0.0 copy-start.4
  130.5 105.1 %shard_map.114 = bf16[2,64,4096]{2,1,0:T(8,128)(2,1)} custom-call(bf16[2048,768]{1,0:T(8,128)(2,1)} %get-tuple-element.4.h_ref, bf16[768,4096]{1,0:T(8,128)(2,1)} %bitcast.10, bf16[64,4096]{1,0:T(8,128)(2,1)} %copy-done.1), custom_call_target="tpu_custom_call" | custom-call | tf_op jit(solution)/shard_map/pallas_call | solution.py:157
  235.6 0.0 copy-done.4
  235.6 0.7 copy.24
  236.3 2.3 copy.26
  (9 shorter events, 0.2 us)
Async XLA Ops:
  0.6 1.0 copy-start
  5.3 17.6 %collective-permute-start.1 = (bf16[64,1024]{1,0:T(8,128)(2,1)}, bf16[64,1024]{1,0:T(8,128)(2,1)S(1)}, u32[]{:S(2)}, u32[]{:S(2)}) collective-permute-start(bf16[64,1024]{1,0:T(8,128)(2,1)} %constant_dynamic-slice_fusion.4), channel_id=1, source_target_pairs={{0,1},{1,0},{2,3},{3,2},{4,5},{5,4},{6,7},{7,6},{8,9},{9,8},{10,11... | collective-permute-start | bytes 393224 | tf_op jit(solution)/shard_map/ppermute | solution.py:397
  11.8 8.7 %copy-start.6 = (s32[128,8]{0,1:T(8,128)S(1)}, s32[128,8]{0,1:T(8,128)}, u32[]{:S(2)}) copy-start(s32[128,8]{0,1:T(8,128)} %param.15) | copy-start | bytes 12292
  11.8 8.8 %copy-start.7 = (f32[128,8]{0,1:T(8,128)S(1)}, f32[128,8]{0,1:T(8,128)}, u32[]{:S(2)}) copy-start(f32[128,8]{0,1:T(8,128)} %param.16) | copy-start | bytes 12292
  11.8 9.1 %copy-start.3 = (bf16[4096,16]{0,1:T(8,128)(2,1)S(1)}, bf16[4096,16]{0,1:T(8,128)(2,1)}, u32[]{:S(2)}) copy-start(bf16[4096,16]{0,1:T(8,128)(2,1)} %param.14) | copy-start | bytes 393220
  11.8 11.1 %collective-permute-start = (bf16[64,1024]{1,0:T(8,128)(2,1)}, bf16[64,1024]{1,0:T(8,128)(2,1)S(1)}, u32[]{:S(2)}, u32[]{:S(2)}) collective-permute-start(bf16[64,1024]{1,0:T(8,128)(2,1)} %constant_dynamic-slice_fusion.5), channel_id=1, source_target_pairs={{0,1},{1,0},{2,3},{3,2},{4,5},{5,4},{6,7},{7,6},{8,9},{9,8},{10,11... | collective-permute-start | bytes 393224 | tf_op jit(solution)/shard_map/ppermute | solution.py:397
  14.8 10.7 %copy-start.2 = (bf16[128,4096]{1,0:T(8,128)(2,1)S(1)}, bf16[128,4096]{1,0:T(8,128)(2,1)}, u32[]{:S(2)}) copy-start(bf16[128,4096]{1,0:T(8,128)(2,1)} %param.11) | copy-start | bytes 3145732
  14.8 10.9 %copy-start.5 = (f32[4096]{0:T(1024)S(1)}, f32[4096]{0:T(1024)}, u32[]{:S(2)}) copy-start(f32[4096]{0:T(1024)} %param.13) | copy-start | bytes 49156
  15.5 7.5 %collective-permute-start.3 = (bf16[64,1024]{1,0:T(8,128)(2,1)}, bf16[64,1024]{1,0:T(8,128)(2,1)S(1)}, u32[]{:S(2)}, u32[]{:S(2)}) collective-permute-start(bf16[64,1024]{1,0:T(8,128)(2,1)} %constant_dynamic-slice_fusion.2), channel_id=1, source_target_pairs={{0,1},{1,0},{2,3},{3,2},{4,5},{5,4},{6,7},{7,6},{8,9},{9,8},{10,11... | collective-permute-start | bytes 393224 | tf_op jit(solution)/shard_map/ppermute | solution.py:397
  20.4 5.0 %collective-permute-start.2 = (bf16[64,1024]{1,0:T(8,128)(2,1)S(1)}, bf16[64,1024]{1,0:T(8,128)(2,1)S(1)}, u32[]{:S(2)}, u32[]{:S(2)}) collective-permute-start(bf16[64,1024]{1,0:T(8,128)(2,1)S(1)} %constant_dynamic-slice_fusion.3), channel_id=1, source_target_pairs={{0,1},{1,0},{2,3},{3,2},{4,5},{5,4},{6,7},{7,6},{8,9},{9,8},{10,11... | collective-permute-start | bytes 393224 | tf_op jit(solution)/shard_map/ppermute | solution.py:397
  25.7 104.8 %copy-start.1 = (bf16[64,4096]{1,0:T(8,128)(2,1)}, bf16[64,4096]{1,0:T(8,128)(2,1)S(1)}, u32[]{:S(2)}) copy-start(bf16[64,4096]{1,0:T(8,128)(2,1)S(1)} %get-tuple-element.13.s_ref) | copy-start | bytes 1572868
  130.5 105.1 %copy-start.4 = (f32[128,16]{1,0:T(8,128)S(1)}, f32[128,16]{1,0:T(8,128)}, u32[]{:S(2)}) copy-start(f32[128,16]{1,0:T(8,128)} %get-tuple-element.11) | copy-start | bytes 24580
